TPU v7x, 256 devices: a whole 4x4x8 slice. The times are simulated.
256 devices in a mesh: ctx: 32 (over y, z_hi, x), tp: 8 (over z_lo, core).
Axes of the slice: x: 4, y: 4, z: 8 (z_hi: 2, z_lo: 4; z = z_hi * 4 + z_lo), core: 2. Of those that a mesh axis runs over, the one named last changes fastest.
Arguments:
- query_raw: bfloat16 [4096, 8192], P('ctx', 'tp'), may hold values from -6 to 6
- key_raw: bfloat16 [4096, 1024], P(('ctx', 'tp')), may hold values from -6 to 6
- values: bfloat16 [4096, 1024], P(('ctx', 'tp')), may hold values from -6 to 6
- grad_out: bfloat16 [4096, 8192], P('ctx', 'tp'), may hold values from -96 to 96
Outputs:
- grad_query: bfloat16 [4096, 8192], P('ctx', 'tp')
- grad_key: bfloat16 [4096, 1024], P(('ctx', 'tp'))
- grad_value: bfloat16 [4096, 1024], P(('ctx', 'tp'))
All inputs are finite; a program needn't handle non-finite values.
Results may differ from a plain program's by a relative error of at most 0.03.
Values may be sent and summed in bfloat16 or wider, within the bound.
A program may use at most 64 MiB of HBM per device.

v0:
```python
import math

import jax
import jax.numpy as jnp
from jax import lax
from jax.sharding import PartitionSpec as P

HEADS = 64
KV_HEADS = 8
HEAD_DIM = 128


epsilon = 1e-06


def unit_rows(raw_values):
    widened = raw_values.astype(jnp.float32)
    factor = lax.rsqrt(jnp.mean(widened * widened, axis=-1, keepdims=True) + epsilon)
    return (widened * factor, factor)


def unit_back(upstream_grad, unit_values, factor):
    return factor * (
        upstream_grad - unit_values * jnp.mean(upstream_grad * unit_values, axis=-1, keepdims=True)
    )


def reorder_rows(matrix, outer_count, inner_count):
    width = matrix.shape[1]
    return (
        matrix.reshape(outer_count, inner_count, -1, width)
        .transpose(1, 0, 2, 3)
        .reshape(matrix.shape)
    )


def split_blocks(key_rows, value_rows):
    key_count = key_rows.shape[0]
    block_len = math.gcd(key_count, 512)
    block_count = key_count // block_len
    key_blocks = key_rows.reshape(block_count, block_len, key_rows.shape[1])
    value_blocks = value_rows.reshape(block_count, block_len, value_rows.shape[1])
    return (key_blocks, value_blocks)


def head_stats(queries, upstream, key_rows, value_rows):
    row_count = queries.shape[0]
    inv_root = 1.0 / math.sqrt(key_rows.shape[1])
    key_blocks, value_blocks = split_blocks(key_rows, value_rows)

    def accumulate(running, pieces):
        key_block, value_block = pieces
        raised = jnp.exp(
            jnp.dot(queries, key_block.T, preferred_element_type=jnp.float32) * inv_root
        )
        value_dots = jnp.dot(upstream, value_block.T, preferred_element_type=jnp.float32)
        return (
            (
                running[0] + jnp.sum(raised, axis=1),
                running[1] + jnp.sum(raised * value_dots, axis=1),
            ),
            None,
        )

    start = jnp.zeros((row_count,), jnp.float32)
    (totals, weighted), unused = lax.scan(accumulate, (start, start), (key_blocks, value_blocks))
    return (totals, weighted)


def head_back(queries, upstream, key_rows, value_rows, totals, delta_row):
    row_count = queries.shape[0]
    key_count = key_rows.shape[0]
    inv_root = 1.0 / math.sqrt(key_rows.shape[1])
    key_blocks, value_blocks = split_blocks(key_rows, value_rows)

    def backward_block(query_acc, pieces):
        key_block, value_block = pieces
        raised = jnp.exp(
            jnp.dot(queries, key_block.T, preferred_element_type=jnp.float32) * inv_root
        )
        attend = raised / totals[:, None]
        attend_cast = attend.astype(jnp.bfloat16)
        value_dots = jnp.dot(upstream, value_block.T, preferred_element_type=jnp.float32)
        score_grad = (attend * (value_dots - delta_row[:, None])).astype(jnp.bfloat16)
        query_acc = (
            query_acc
            + jnp.dot(score_grad, key_block, preferred_element_type=jnp.float32) * inv_root
        )
        key_piece = jnp.dot(score_grad.T, queries, preferred_element_type=jnp.float32) * inv_root
        value_piece = jnp.dot(attend_cast.T, upstream, preferred_element_type=jnp.float32)
        return (query_acc, (key_piece, value_piece))

    query_grad, (key_grad, value_grad) = lax.scan(
        backward_block,
        jnp.zeros((row_count, queries.shape[1]), jnp.float32),
        (key_blocks, value_blocks),
    )
    return (query_grad, key_grad.reshape(key_count, -1), value_grad.reshape(key_count, -1))


def head_grad(queries, upstream, key_rows, value_rows):
    totals, weighted = head_stats(queries, upstream, key_rows, value_rows)
    return head_back(queries, upstream, key_rows, value_rows, totals, weighted / totals)


def by_heads(rows, row_count, local_heads, group_size):
    return (
        rows.reshape(row_count, local_heads, group_size, HEAD_DIM)
        .transpose(1, 0, 2, 3)
        .reshape(local_heads, row_count * group_size, HEAD_DIM)
    )


def shards(query_raw, key_raw, values, grad_out):
    ctx_count = lax.axis_size("ctx")
    tp_count = lax.axis_size("tp")
    text_rows = query_raw.shape[0]
    group_size = HEADS // KV_HEADS
    local_heads = query_raw.shape[1] // (group_size * HEAD_DIM)
    local_width = local_heads * HEAD_DIM
    image_total = key_raw.shape[0] * ctx_count * tp_count
    query_unit, query_scale = unit_rows(
        query_raw.reshape(text_rows, local_heads, group_size, HEAD_DIM)
    )
    query_cast = query_unit.astype(jnp.bfloat16)
    queries = query_cast.transpose(1, 0, 2, 3).reshape(
        local_heads, text_rows * group_size, HEAD_DIM
    )
    upstream = by_heads(grad_out, text_rows, local_heads, group_size)
    raw_keys, raw_values = (
        lax.all_gather(key_raw, "ctx", axis=0, tiled=True),
        lax.all_gather(values, "ctx", axis=0, tiled=True),
    )
    raw_keys, raw_values = (
        lax.all_to_all(raw_keys, "tp", split_axis=1, concat_axis=0, tiled=True),
        lax.all_to_all(raw_values, "tp", split_axis=1, concat_axis=0, tiled=True),
    )
    raw_keys = reorder_rows(raw_keys, tp_count, ctx_count)
    value_all = reorder_rows(raw_values, tp_count, ctx_count)
    key_unit, key_scale = unit_rows(raw_keys.reshape(image_total, local_heads, HEAD_DIM))
    key_all = key_unit.astype(jnp.bfloat16).reshape(image_total, local_width)
    key_heads = key_all.reshape(image_total, local_heads, HEAD_DIM).transpose(1, 0, 2)
    value_heads = value_all.reshape(image_total, local_heads, HEAD_DIM).transpose(1, 0, 2)
    query_grad, key_grad, value_grad = lax.map(
        lambda bundle: head_grad(bundle[0], bundle[1], bundle[2], bundle[3]),
        (queries, upstream, key_heads, value_heads),
    )
    query_grad = query_grad.reshape(local_heads, text_rows, group_size, HEAD_DIM).transpose(
        1, 0, 2, 3
    )
    grad_query = (
        unit_back(query_grad, query_unit, query_scale)
        .astype(jnp.bfloat16)
        .reshape(text_rows, local_heads * group_size * HEAD_DIM)
    )
    key_grad = key_grad.transpose(1, 0, 2)
    value_grad = value_grad.transpose(1, 0, 2).reshape(image_total, local_width)
    key_part = unit_back(key_grad, key_unit, key_scale).reshape(image_total, local_width)
    key_part = reorder_rows(key_part, ctx_count, tp_count)
    value_part = reorder_rows(value_grad, ctx_count, tp_count)
    key_part, value_part = (
        lax.all_to_all(
            key_part.astype(jnp.bfloat16), "tp", split_axis=0, concat_axis=1, tiled=True
        ).astype(key_part.dtype),
        lax.all_to_all(
            value_part.astype(jnp.bfloat16), "tp", split_axis=0, concat_axis=1, tiled=True
        ).astype(value_part.dtype),
    )
    key_sum, value_sum = (
        lax.psum_scatter(
            key_part.astype(jnp.bfloat16), "ctx", scatter_dimension=0, tiled=True
        ).astype(jnp.float32),
        lax.psum_scatter(
            value_part.astype(jnp.bfloat16), "ctx", scatter_dimension=0, tiled=True
        ).astype(jnp.float32),
    )
    grad_key = key_sum.astype(jnp.bfloat16)
    grad_value = value_sum.astype(jnp.bfloat16)
    return (grad_query, grad_key, grad_value)


def solution(mesh):
    return jax.shard_map(
        shards,
        mesh=mesh,
        in_specs=(P("ctx", "tp"), P(("ctx", "tp"), None), P(("ctx", "tp"), None), P("ctx", "tp")),
        out_specs=(P("ctx", "tp"), P(("ctx", "tp"), None), P(("ctx", "tp"), None)),
        check_vma=False,
    )
```

profile of v0, /device:TPU:32, one launch (start us, length us, event | category | flops | bytes accessed | tf_op | source)
XLA Modules:
  0.0 791.3 jit_solution(11506440971057090133)
XLA Ops:
  8.6 85.6 %all-gather.3.cloned.1.call-done = bf16[512,1024]{1,0:T(8,128)(2,1)} async-done(((bf16[16,1024]{1,0:T(8,128)(2,1)}), bf16[512,1024]{1,0:T(8,128)(2,1)}) %all-gather.3.cloned.1.call-update) | async-done | bytes 1048592 | tf_op jit(solution)/shard_map/all_gather | solution.py:131
  94.2 2.3 copy.48
  96.5 5.5 all-to-all-start
  102.1 71.7 %all-gather.5.cloned.1.call-done = bf16[512,1024]{1,0:T(8,128)(2,1)} async-done(((bf16[16,1024]{1,0:T(8,128)(2,1)}), bf16[512,1024]{1,0:T(8,128)(2,1)}) %all-gather.5.cloned.1.call-update) | async-done | bytes 1048592 | tf_op jit(solution)/shard_map/all_gather | solution.py:132
  173.8 2.3 copy.52
  176.1 6.2 all-to-all-start.1
  184.2 1.6 convert_bitcast_fusion
  185.9 1.9 copy.49
  187.8 1.6 copy.50
  190.7 14.7 %all-to-all-done.1 = bf16[512,8,128]{0,2,1:T(8,128)(2,1)} async-done(((bf16[512,8,128]{0,2,1:T(8,128)(2,1)}), bf16[512,8,128]{0,2,1:T(8,128)(2,1)}, u32[]{:S(2)}, u32[]{:S(2)}) %all-to-all-start.1) | async-done | bytes 1048608 | tf_op jit(solution)/shard_map/all_to_all | solution.py:136
  205.4 2.3 copy.53
  207.7 2.5 copy.54
  212.0 2.8 multiply_convert_fusion.1
  214.8 27.4 %while.43 = (s32[]{:T(128)}, f32[1024]{0:T(1024)}, f32[1024]{0:T(1024)}, bf16[8,512,128]{2,1,0:T(8,128)(2,1)}, bf16[1024,128]{1,0:T(8,128)(2,1)S(1)}, /*index=5*...) while((s32[]{:T(128)}, f32[1024]{0:T(1024)}, f32[1024]{0:T(1024)}, ...), condition=%wide.region_5.6_spmd.clone, body=%wide.region_2.5_spmd.clone.sunk | while | flops 271058944 | bytes 5079271 | solution.py:66
  242.9 51.9 %while.44 = (s32[]{:T(128)}, f32[1024,128]{1,0:T(8,128)S(1)}, f32[8,512,128]{2,1,0:T(8,128)}, bf16[8,512,128]{2,1,0:T(8,128)(2,1)}, bf16[8,512,128]{2,1,0:T(8,12...) while((s32[]{:T(128)}, f32[1024,128]{1,0:T(8,128)S(1)}, ...), condition=%wide.region_7.8_spmd.clone, body=%wide.region_6.7_spmd.clone.sunk | while | flops 674693120 | bytes 12460187 | solution.py:93
  294.8 2.4 copy.58
  297.2 7.7 all-to-all-start.3
  304.9 2.8 multiply_reduce_fusion.1
  307.9 4.0 fusion.23
  312.0 16.1 %all-to-all-done.3 = bf16[8,512,128]{2,1,0:T(8,128)(2,1)} async-done(((bf16[8,512,128]{2,1,0:T(8,128)(2,1)}), bf16[8,512,128]{2,1,0:T(8,128)(2,1)}, u32[]{:S(2)}, u32[]{:S(2)}) %all-to-all-start.3) | async-done | bytes 1048608 | tf_op jit(solution)/shard_map/all_to_all | solution.py:165
  328.1 7.1 all-to-all-start.2
  338.0 21.6 %all-to-all-done.2 = bf16[8,512,128]{2,1,0:T(8,128)(2,1)S(1)} async-done(((bf16[8,512,128]{2,1,0:T(8,128)(2,1)}), bf16[8,512,128]{2,1,0:T(8,128)(2,1)S(1)}, u32[]{:S(2)}, u32[]{:S(2)}) %all-to-all-start.2) | async-done | bytes 1048608 | tf_op jit(solution)/shard_map/all_to_all | solution.py:162
  363.0 200.4 %reduce-scatter.7.cloned.1.call-done = bf16[16,1024]{1,0:T(8,128)(2,1)} async-done(((bf16[512,1024]{1,0:T(8,128)(2,1)}), bf16[16,1024]{1,0:T(8,128)(2,1)}) %reduce-scatter.7.cloned.1.call-update) | async-done | bytes 32784
  563.4 221.4 %reduce-scatter.5.cloned.1.call-done = bf16[16,1024]{1,0:T(8,128)(2,1)} async-done(((bf16[512,1024]{1,0:T(8,128)(2,1)}), bf16[16,1024]{1,0:T(8,128)(2,1)}) %reduce-scatter.5.cloned.1.call-update) | async-done | bytes 32784 | tf_op jit(solution)/shard_map/reduce_scatter | solution.py:170
  (190 shorter events, 92.0 us)
Async XLA Ops:
  7.2 87.1 %all-gather.3.cloned.1.call-start = ((), (), s32[]{:S(2)}) async-start(), calls=%async_computation.6 | async-start | bytes 1081344 | tf_op jit(solution)/shard_map/all_gather | solution.py:131
  7.9 165.9 %all-gather.5.cloned.1.call-start = ((), (), s32[]{:S(2)}) async-start(), calls=%async_computation.7 | async-start | bytes 1081344 | tf_op jit(solution)/shard_map/all_gather | solution.py:132
  96.5 79.5 %all-to-all-start = ((bf16[512,8,128]{0,2,1:T(8,128)(2,1)}), bf16[512,8,128]{0,2,1:T(8,128)(2,1)S(1)}, u32[]{:S(2)}, u32[]{:S(2)}) async-start(bf16[512,8,128]{0,2,1:T(8,128)(2,1)} %bitcast), calls=%async_computation | async-start | bytes 2097152 | tf_op jit(solution)/shard_map/all_to_all | solution.py:135
  102.1 80.2 %copy-start.6 = (bf16[128,1024]{1,0:T(8,128)(2,1)S(1)}, bf16[128,1024]{1,0:T(8,128)(2,1)}, u32[]{:S(2)}) copy-start(bf16[128,1024]{1,0:T(8,128)(2,1)} %param.11) | copy-start | bytes 786436
  102.1 80.4 %copy-start.2 = (bf16[128,1024]{1,0:T(8,128)(2,1)S(1)}, bf16[128,1024]{1,0:T(8,128)(2,1)}, u32[]{:S(2)}) copy-start(bf16[128,1024]{1,0:T(8,128)(2,1)} %param.8) | copy-start | bytes 786436
  176.1 29.3 %all-to-all-start.1 = ((bf16[512,8,128]{0,2,1:T(8,128)(2,1)}), bf16[512,8,128]{0,2,1:T(8,128)(2,1)}, u32[]{:S(2)}, u32[]{:S(2)}) async-start(bf16[512,8,128]{0,2,1:T(8,128)(2,1)} %bitcast.6), calls=%async_computation.1 | async-start | bytes 2097152 | tf_op jit(solution)/shard_map/all_to_all | solution.py:136
  212.0 2.8 copy-start.7
  214.8 2.8 copy-start.9
  214.8 2.8 copy-start.11
  218.2 2.8 copy-start.11
  221.6 2.8 copy-start.9
  221.7 2.8 copy-start.11
  225.1 2.8 copy-start.11
  228.5 2.8 copy-start.11
  231.9 2.8 copy-start.11
  235.3 2.8 copy-start.11
  238.8 2.8 copy-start.11
  294.8 10.1 %copy-start.8 = (f32[8,512]{1,0:T(8,128)S(1)}, f32[8,512]{1,0:T(8,128)}, u32[]{:S(2)}) copy-start(f32[8,512]{1,0:T(8,128)} %copy-done.7) | copy-start | bytes 49156
  297.2 30.9 %all-to-all-start.3 = ((bf16[8,512,128]{2,1,0:T(8,128)(2,1)}), bf16[8,512,128]{2,1,0:T(8,128)(2,1)}, u32[]{:S(2)}, u32[]{:S(2)}) async-start(bf16[8,512,128]{2,1,0:T(8,128)(2,1)} %bitcast.118), calls=%async_computation.4 | async-start | bytes 2097152 | tf_op jit(solution)/shard_map/all_to_all | solution.py:165
  328.1 31.6 %all-to-all-start.2 = ((bf16[8,512,128]{2,1,0:T(8,128)(2,1)}), bf16[8,512,128]{2,1,0:T(8,128)(2,1)S(1)}, u32[]{:S(2)}, u32[]{:S(2)}) async-start(bf16[8,512,128]{2,1,0:T(8,128)(2,1)} %bitcast.121), calls=%async_computation.2 | async-start | bytes 2097152 | tf_op jit(solution)/shard_map/all_to_all | solution.py:162
  335.1 228.3 %reduce-scatter.7.cloned.1.call-start = ((), (), s32[]{:S(2)}) async-start(), calls=%async_computation.9 | async-start | bytes 1081344
  338.0 22.9 %copy-start.1 = (f32[1024,128]{1,0:T(8,128)S(1)}, f32[1024,128]{1,0:T(8,128)}, u32[]{:S(2)}) copy-start(f32[1024,128]{1,0:T(8,128)} %copy-done) | copy-start | bytes 1572868
  338.0 22.9 %copy-start.14 = (f32[1024]{0:T(1024)S(1)}, f32[1024]{0:T(1024)}, u32[]{:S(2)}) copy-start(f32[1024]{0:T(1024)} %copy-done.13) | copy-start | bytes 12292
  338.0 446.8 %reduce-scatter.5.cloned.1.call-start = ((), (), s32[]{:S(2)}) async-start(), calls=%async_computation.8 | async-start | bytes 1081344 | tf_op jit(solution)/shard_map/reduce_scatter | solution.py:170
  (27 other events, 32.1 us)
Sparse Core Ops, SparseCore 0:
  11.4 82.7 all-gather.2
  97.6 76.0 all-gather.4
  339.0 224.3 reduce-scatter.6
  566.5 218.2 reduce-scatter.4
where the time goes:
time: 793 us; the launch traced here: 791 us
  waiting for transfers between devices  633 us (80%)
  matrix products  73.8 us (9%)
  local copies, waits for them, and re-layouts  28.1 us (4%)
  starting transfers between devices  26.7 us (3%)
  other arithmetic  15.1 us (2%)
  between operations  14 us (2%)
    reduce_scatter x1, waiting for transfers between devices, shards(): lax.psum_scatter(key_part.astype(jnp.bfloat16), 'ctx', scatter_dimension=...  221 us
    unnamed x5, waiting for transfers between devices  202 us
    all_gather x1, waiting for transfers between devices, shards(): lax.all_gather(key_raw, 'ctx', axis=0, tiled=True)  85.6 us
    all_gather x1, waiting for transfers between devices, shards(): lax.all_gather(values, 'ctx', axis=0, tiled=True)  71.7 us
    all_to_all x1, waiting for transfers between devices, shards(): lax.all_to_all(key_part.astype(jnp.bfloat16), 'tp', split_axis=0, concat_...  21.6 us
    all_to_all x1, waiting for transfers between devices, shards(): lax.all_to_all(value_part.astype(jnp.bfloat16), 'tp', split_axis=0, conca...  16.1 us
  transfers between devices with their start and end apart: 8, of which 7 were waited for; matrix products, arithmetic and copies ran while one was open for 3% of the time, Pallas kernels for 0%

commit v1 on v0

v1 whole, which is shorter than its diff:
```python
import math

import jax
import jax.numpy as jnp
from jax import lax
from jax.experimental import pallas as pl
from jax.experimental.pallas import tpu as pltpu
from jax.sharding import PartitionSpec as P

F32 = jnp.float32
BF16 = jnp.bfloat16
MESH = pl.DeviceIdType.MESH
EPS = 1e-6
D = 128
HEADS = 8
ROWS = 1024
BLOCK = 256
HALF = BLOCK // 2
LINE = 16
INV = 1.0 / math.sqrt(D)
EXP2 = INV * math.log2(math.e)

ORDER = (
    ((0, 0),),
    ((1, 0), (3, 0), (0, 1), (0, 3)),
    ((1, 1), (1, 3), (3, 1), (3, 3)),
    ((2, 0), (0, 2)),
    ((1, 2), (3, 2), (2, 1), (2, 3)),
    ((2, 2),),
)
PLACE = {at: n for n, at in enumerate(sum(ORDER, ()))}
GROUPS = []
for group in ORDER:
    GROUPS.append((PLACE[group[0]], PLACE[group[-1]] + 1))


def unit(raw):
    scale = lax.rsqrt(jnp.mean(raw * raw, axis=-1, keepdims=True) + EPS)
    return raw * scale, scale


def unit_back(grad, unit_rows, scale):
    return scale * (grad - unit_rows * jnp.mean(grad * unit_rows, axis=-1, keepdims=True))


def place(kind, a, b):
    a, b = a % 4, b % 4
    return PLACE[(a, b) if kind == 0 else (b, a)]


def kernel(
    q_ref, k_ref, v_ref, do_ref,
    gq_ref, gk_ref, gv_ref,
    q_t, do_t, q_n, do_n, raised, dots, totals, weighted, rows, dq_t,
    mine, kv, part, piece_in, full_in, last_piece, last_full, line_in,
    z_send, z_recv, y_send, y_recv, send, recv, r_send, p_recv, f_recv, lp_recv, lf_recv,
):
    ctx = lax.axis_index("ctx")
    tp = lax.axis_index("tp")
    y, z_hi, x = ctx // 8, (ctx // 4) % 2, ctx % 4
    me = z_hi * 8 + tp

    def beside(axis, step):
        if axis == 0:
            return (y * 8 + z_hi * 4 + (x + step) % 4, tp)
        return (((y + step) % 4) * 8 + z_hi * 4 + x, tp)

    def on_line(step):
        other = (me + step) % LINE
        return (y * 8 + (other // 8) * 4 + x, other % 8)

    barrier = pltpu.get_barrier_semaphore()

    def greet(step, carry):
        pl.semaphore_signal(barrier, inc=1, device_id=on_line(step), device_id_type=MESH)
        return carry

    lax.fori_loop(1, LINE, greet, 0)
    for axis in range(2):
        for step in (1, 3):
            pl.semaphore_signal(barrier, inc=1, device_id=beside(axis, step), device_id_type=MESH)

    for h in range(HEADS):
        cols = slice(h * D, (h + 1) * D)
        mine[h, 0] = unit(k_ref[:, cols].astype(F32))[0].astype(BF16)
        mine[h, 1] = v_ref[:, cols]
    pl.semaphore_wait(barrier, LINE - 1 + 4)

    def z_copy(step):
        target = on_line(step)
        spot = pl.multiple_of((LINE - step) * 16, 16)
        return pltpu.make_async_remote_copy(
            src_ref=mine.at[target[1]],
            dst_ref=kv.at[0, :, pl.ds(spot, 16), :],
            send_sem=z_send.at[step],
            recv_sem=z_recv.at[step],
            device_id=target,
            device_id_type=MESH,
        )

    def z_start(step, carry):
        z_copy(step).start()
        return carry

    lax.fori_loop(1, LINE, z_start, 0)
    kv[0, :, 0:16, :] = mine[tp]

    for h in range(HEADS):
        cols = slice(h * D, (h + 1) * D)
        cast = unit(q_ref[:, cols].astype(F32))[0].astype(BF16)
        q_n[cols, :] = cast
        q_t[:, cols] = cast.T
        do_n[cols, :] = do_ref[:, cols]
        do_t[:, cols] = do_ref[:, cols].T
    totals[...] = jnp.zeros_like(totals)
    weighted[...] = jnp.zeros_like(weighted)
    dq_t[...] = jnp.zeros_like(dq_t)

    def z_wait(step, carry):
        copy = z_copy(step)
        copy.wait_send()
        copy.wait_recv()
        return carry

    lax.fori_loop(1, LINE, z_wait, 0)

    def pass_1(n, carry):
        scores = jnp.dot(kv[n, 0], q_t[...], preferred_element_type=F32)
        value_dots = jnp.dot(kv[n, 1], do_t[...], preferred_element_type=F32)
        e = jnp.exp2(scores * EXP2)
        raised[n] = e
        dots[n] = value_dots
        totals[...] += jnp.sum(e.reshape(BLOCK // 8, 8, ROWS), axis=0)
        weighted[...] += jnp.sum((e * value_dots).reshape(BLOCK // 8, 8, ROWS), axis=0)
        return carry

    started = []

    def rows_of(half):
        return slice(0, BLOCK) if half is None else slice(half * HALF, (half + 1) * HALF)

    def gather_copy(kind, a, b, axis_of, step, half):
        src = place(kind, a, b)
        dst = place(kind, a - step, b) if axis_of == 0 else place(kind, a, b - step)
        axis = axis_of if kind == 0 else 1 - axis_of
        return pltpu.make_async_remote_copy(
            src_ref=kv.at[src, kind, rows_of(half), :],
            dst_ref=kv.at[dst, kind, rows_of(half), :],
            send_sem=send.at[len(started)],
            recv_sem=recv.at[dst, kind, half or 0],
            device_id=beside(axis, step % 4),
            device_id_type=MESH,
        )

    def forward(a, b, axis_of, step, half=None):
        for kind in range(2):
            copy = gather_copy(kind, a, b, axis_of, step, half)
            copy.start()
            started.append(copy)

    def arrived(a, b, half=None):
        for kind in range(2):
            at = place(kind, a, b)
            ref = kv.at[at, kind, rows_of(half), :]
            pltpu.make_async_copy(ref, ref, recv.at[at, kind, half or 0]).wait()

    def run(body, group):
        lax.fori_loop(*GROUPS[group], body, 0)

    for axis_of in range(2):
        for step in (1, -1):
            forward(0, 0, axis_of, step)
    run(pass_1, 0)
    for a in (1, 3):
        arrived(a, 0)
        forward(a, 0, 0, a - 2, half=1 if a == 1 else 0)
    for a in (1, 3):
        for step in (1, -1):
            forward(a, 0, 1, step)
    arrived(0, 1)
    forward(0, 1, 1, -1, half=1)
    arrived(0, 3)
    forward(0, 3, 1, 1, half=0)
    run(pass_1, 1)
    arrived(2, 0, 0)
    arrived(2, 0, 1)
    for step in (1, -1):
        forward(2, 0, 1, step)
    for a in (1, 3):
        arrived(a, 1)
        forward(a, 1, 1, -1, half=1)
        arrived(a, 3)
        forward(a, 3, 1, 1, half=0)
    run(pass_1, 2)
    arrived(0, 2, 0)
    arrived(0, 2, 1)
    arrived(2, 1)
    forward(2, 1, 1, -1, half=1)
    arrived(2, 3)
    forward(2, 3, 1, 1, half=0)
    run(pass_1, 3)
    for a in (1, 3):
        arrived(a, 2, 0)
        arrived(a, 2, 1)
    run(pass_1, 4)
    arrived(2, 2, 0)
    arrived(2, 2, 1)
    run(pass_1, 5)
    for copy in started:
        copy.wait_send()

    total = jnp.sum(totals[...], axis=0, keepdims=True)
    inverse = 1.0 / total
    rows[0:1, :] = inverse
    rows[1:2, :] = jnp.sum(weighted[...], axis=0, keepdims=True) * inverse

    def pass_2(n, carry):
        attend = raised[n] * rows[0:1, :]
        score_grad = (attend * (dots[n] - rows[1:2, :])).astype(BF16)
        part[n, 1] = jnp.dot(attend.astype(BF16), do_n[...], preferred_element_type=F32).astype(BF16)
        part[n, 0] = (jnp.dot(score_grad, q_n[...], preferred_element_type=F32) * INV).astype(BF16)
        dq_t[...] += jnp.dot(kv[n, 0].T, score_grad, preferred_element_type=F32)
        return carry

    sent = []

    def give(kind, src, dst, sem, axis, step):
        copy = pltpu.make_async_remote_copy(
            src_ref=src,
            dst_ref=dst,
            send_sem=r_send.at[len(sent)],
            recv_sem=sem,
            device_id=beside(axis, step % 4),
            device_id_type=MESH,
        )
        copy.start()
        sent.append(copy)

    def take(ref, sem):
        pltpu.make_async_copy(ref, ref, sem).wait()

    def add(at, kind, half, *refs):
        where = (at, kind, rows_of(half), slice(None))
        value = part[where].astype(F32)
        for ref in refs:
            value = value + ref[...].astype(F32)
        part[where] = value.astype(BF16)

    def far(a, b, axis_of, pieces, sems, index):
        for kind in range(2):
            axis = axis_of if kind == 0 else 1 - axis_of
            at = place(kind, a, b)
            for half, step in ((0, 1), (1, -1)):
                give(kind, part.at[at, kind, rows_of(half), :], pieces.at[(kind, *index, half)],
                     sems.at[(kind, *index, half)], axis, step)

    def near(a, b, axis_of, step, pieces, p_sems, fulls, f_sems, index):
        half = 0 if step == 1 else 1
        for kind in range(2):
            axis = axis_of if kind == 0 else 1 - axis_of
            at = place(kind, a, b)
            take(pieces.at[(kind, *index, half)], p_sems.at[(kind, *index, half)])
            add(at, kind, half, pieces.at[(kind, *index, half)])
            give(kind, part.at[at, kind], fulls.at[(kind, *index, half)], f_sems.at[(kind, *index, half)], axis, step)

    def own(a, b, fulls, f_sems, index):
        for kind in range(2):
            at = place(kind, a, b)
            for side in range(2):
                take(fulls.at[(kind, *index, side)], f_sems.at[(kind, *index, side)])
            add(at, kind, None, fulls.at[(kind, *index, 0)], fulls.at[(kind, *index, 1)])

    def far_1(a):
        far(a, 2, 1, piece_in, p_recv, (a,))

    def near_1(a, b):
        near(a, b, 1, 1 if b == 1 else -1, piece_in, p_recv, full_in, f_recv, (a,))

    def own_1(a):
        own(a, 0, full_in, f_recv, (a,))

    run(pass_2, 5)
    far_1(2)
    run(pass_2, 4)
    far_1(1)
    far_1(3)
    near_1(2, 1)
    near_1(2, 3)
    run(pass_2, 3)
    far_1(0)
    run(pass_2, 2)
    for a in (1, 3):
        for b in (1, 3):
            near_1(a, b)
    own_1(2)
    far(2, 0, 0, last_piece, lp_recv, ())
    run(pass_2, 1)
    near_1(0, 1)
    near_1(0, 3)
    run(pass_2, 0)
    for a in (1, 3):
        own_1(a)
        near(a, 0, 0, 1 if a == 1 else -1, last_piece, lp_recv, last_full, lf_recv, ())

    for h in range(HEADS):
        cols = slice(h * D, (h + 1) * D)
        unit_rows, scale = unit(q_ref[:, cols].astype(F32))
        gq_ref[:, cols] = unit_back(dq_t[:, cols].T * INV, unit_rows, scale).astype(BF16)

    own_1(0)
    own(0, 0, last_full, lf_recv, ())

    def line_copy(step):
        spot = pl.multiple_of(step * 16, 16)
        return pltpu.make_async_remote_copy(
            src_ref=part.at[0, :, pl.ds(spot, 16), :],
            dst_ref=line_in.at[me],
            send_sem=y_send.at[step],
            recv_sem=y_recv.at[step],
            device_id=on_line(step),
            device_id_type=MESH,
        )

    def line_start(step, carry):
        line_copy(step).start()
        return carry

    lax.fori_loop(1, LINE, line_start, 0)
    line_in[me] = part[0, :, 0:16, :]
    for copy in sent:
        copy.wait_send()

    def line_wait(step, carry):
        copy = line_copy(step)
        copy.wait_send()
        came = line_in.at[(me + LINE - step) % LINE]
        pltpu.make_async_copy(came, came, y_recv.at[step]).wait()
        return carry

    lax.fori_loop(1, LINE, line_wait, 0)
    for h in range(HEADS):
        cols = slice(h * D, (h + 1) * D)
        sums = line_in[h].astype(F32) + line_in[h + 8].astype(F32)
        unit_rows, scale = unit(k_ref[:, cols].astype(F32))
        gk_ref[:, cols] = unit_back(sums[0], unit_rows, scale).astype(BF16)
        gv_ref[:, cols] = sums[1].astype(BF16)


def shards(query_raw, key_raw, values, grad_out):
    vmem = pl.BlockSpec(memory_space=pltpu.VMEM)
    dma = pltpu.SemaphoreType.DMA
    return pl.pallas_call(
        kernel,
        out_shape=[
            jax.ShapeDtypeStruct(query_raw.shape, BF16),
            jax.ShapeDtypeStruct(key_raw.shape, BF16),
            jax.ShapeDtypeStruct(values.shape, BF16),
        ],
        in_specs=[vmem] * 4,
        out_specs=[vmem] * 3,
        scratch_shapes=[
            pltpu.VMEM((D, ROWS), BF16),
            pltpu.VMEM((D, ROWS), BF16),
            pltpu.VMEM((ROWS, D), BF16),
            pltpu.VMEM((ROWS, D), BF16),
            pltpu.VMEM((16, BLOCK, ROWS), F32),
            pltpu.VMEM((16, BLOCK, ROWS), F32),
            pltpu.VMEM((8, ROWS), F32),
            pltpu.VMEM((8, ROWS), F32),
            pltpu.VMEM((8, ROWS), F32),
            pltpu.VMEM((D, ROWS), F32),
            pltpu.VMEM((HEADS, 2, 16, D), BF16),
            pltpu.VMEM((16, 2, BLOCK, D), BF16),
            pltpu.VMEM((16, 2, BLOCK, D), BF16),
            pltpu.VMEM((2, 4, 2, HALF, D), BF16),
            pltpu.VMEM((2, 4, 2, BLOCK, D), BF16),
            pltpu.VMEM((2, 2, HALF, D), BF16),
            pltpu.VMEM((2, 2, BLOCK, D), BF16),
            pltpu.VMEM((LINE, 2, 16, D), BF16),
            dma((LINE,)),
            dma((LINE,)),
            dma((LINE,)),
            dma((LINE,)),
            dma((40,)),
            dma((16, 2, 2)),
            dma((40,)),
            dma((2, 4, 2)),
            dma((2, 4, 2)),
            dma((2, 2)),
            dma((2, 2)),
        ],
        compiler_params=pltpu.CompilerParams(
            collective_id=0, has_side_effects=True, vmem_limit_bytes=56 * 2**20
        ),
    )(query_raw, key_raw, values, grad_out)


def solution(mesh):
    split = (P("ctx", "tp"), P(("ctx", "tp"), None), P(("ctx", "tp"), None), P("ctx", "tp"))
    return jax.shard_map(
        shards, mesh=mesh, in_specs=split, out_specs=split[:3], check_vma=False
    )
```

time: 793 us -> 64.5 us (0.08)
  the two profiles are of different devices: /device:TPU:32 before, /device:TPU:1 now
where the time goes in v1:
time: 64.5 us; the launch traced here: 64.3 us
  Pallas kernels  60.6 us (94%)
  local copies, waits for them, and re-layouts  3.06 us (5%)
  between operations  0.65 us (1%)
    pallas_call x1, Pallas kernels, shards(): pl.pallas_call(kernel, out_shape=[jax.ShapeDtypeStruct(query_raw.shape, B...  60.6 us
    unnamed x7, local copies, waits for them, and re-layouts  3.06 us

profile of v1, /device:TPU:1, one launch (start us, length us, event | category | flops | bytes accessed | tf_op | source)
XLA Modules:
  0.0 64.3 jit_solution(8404734684239090446)
XLA Ops:
  0.6 60.6 %shard_map.67 = (bf16[128,1024]{1,0:T(8,128)(2,1)}, bf16[16,1024]{1,0:T(8,128)(2,1)}, bf16[16,1024]{1,0:T(8,128)(2,1)}) custom-call(bf16[128,1024]{1,0:T(8,128)(2,1)} %q_ref.1, bf16[16,1024]{1,0:T(8,128)(2,1)} %k_ref.1, bf16[16,1024]{1,0:T(8,128)(2,1)} %v_ref.1, bf16[128,1024]{1,0:T(8,128)(2,1)} %do_ref.1), custom_call_target="tpu_custom_call" | custom-call | tf_op jit(solution)/shard_map/pallas_call | solution.py:352
  61.2 0.0 copy-start.1
  61.2 1.7 %copy.10 = bf16[128,1024]{1,0:T(8,128)(2,1)} copy(bf16[128,1024]{1,0:T(8,128)(2,1)} %get-tuple-element.6) | data formatting | bytes 524288
  62.9 0.0 copy-done.1
  62.9 0.0 copy-start
  62.9 0.6 copy.11
  63.5 0.2 copy-done
  63.7 0.6 copy.12
Async XLA Ops:
  61.2 1.7 %copy-start.1 = (bf16[16,1024]{1,0:T(8,128)(2,1)S(1)}, bf16[16,1024]{1,0:T(8,128)(2,1)}, u32[]{:S(2)}) copy-start(bf16[16,1024]{1,0:T(8,128)(2,1)} %get-tuple-element.7) | copy-start | bytes 98308
  62.9 0.8 %copy-start = (bf16[16,1024]{1,0:T(8,128)(2,1)S(1)}, bf16[16,1024]{1,0:T(8,128)(2,1)}, u32[]{:S(2)}) copy-start(bf16[16,1024]{1,0:T(8,128)(2,1)} %get-tuple-element.8) | copy-start | bytes 98308

commit v2 on v1

v2 whole, which is shorter than its diff:
```python
import math

import jax
import jax.numpy as jnp
from jax import lax
from jax.experimental import pallas as pl
from jax.experimental.pallas import tpu as pltpu
from jax.sharding import PartitionSpec as P

F32 = jnp.float32
BF16 = jnp.bfloat16
MESH = pl.DeviceIdType.MESH
EPS = 1e-6
D = 128
HEADS = 8
ROWS = 1024
BLOCK = 256
HALF = BLOCK // 2
LINE = 16
INV = 1.0 / math.sqrt(D)
EXP2 = INV * math.log2(math.e)
KEYS, VALUES = 0, 1

ORDER = (
    ((0, 0),),
    ((1, 0), (3, 0), (0, 1), (0, 3)),
    ((1, 1), (1, 3), (3, 1), (3, 3)),
    ((2, 0), (0, 2)),
    ((1, 2), (3, 2), (2, 1), (2, 3)),
    ((2, 2),),
)
PLACE = {at: n for n, at in enumerate(sum(ORDER, ()))}
GROUPS = [(PLACE[group[0]], PLACE[group[-1]] + 1) for group in ORDER]
FAR_FIRST = (8, 7, 9, 6, 10, 5, 11, 4, 12, 3, 13, 2, 14, 15, 1)

G_FIRST = 1
G_SECOND = 4
R_FIRST = 1
R_SECOND = 0


def unit(raw):
    scale = lax.rsqrt(jnp.mean(raw * raw, axis=-1, keepdims=True) + EPS)
    return raw * scale, scale


def unit_back(grad, unit_rows, scale):
    return scale * (grad - unit_rows * jnp.mean(grad * unit_rows, axis=-1, keepdims=True))


def place(kind, a, b):
    a, b = a % 4, b % 4
    return PLACE[(a, b) if kind == KEYS else (b, a)]


def rows_of(half):
    return slice(0, BLOCK) if half is None else slice(half * HALF, (half + 1) * HALF)


def kernel(
    q_in, k_ref, v_ref, do_in,
    gq_ref, gk_ref, gv_ref,
    q_ref, do_ref, q_t, do_t, q_n, do_n, raised, dots, totals, weighted, rows, dq_t,
    mine, kv, part, piece_in, full_in, last_piece, last_full, line_in,
    load, z_sem, y_sem, send, recv, r_send, p_recv, f_recv, l_recv,
):
    ctx = lax.axis_index("ctx")
    tp = lax.axis_index("tp")
    y, z_hi, x = ctx // 8, (ctx // 4) % 2, ctx % 4
    me = z_hi * 8 + tp

    def beside(kind, axis, step):
        if axis == kind:
            return (y * 8 + z_hi * 4 + (x + step) % 4, tp)
        return (((y + step) % 4) * 8 + z_hi * 4 + x, tp)

    def on_line(step):
        other = (me + step) % LINE
        return (y * 8 + (other // 8) * 4 + x, other % 8)

    def take(ref, sem):
        pltpu.make_async_copy(ref, ref, sem).wait()

    q_load = pltpu.make_async_copy(q_in, q_ref, load.at[0])
    do_load = pltpu.make_async_copy(do_in, do_ref, load.at[1])
    q_load.start()
    do_load.start()
    barrier = pltpu.get_barrier_semaphore()
    for step in FAR_FIRST:
        pl.semaphore_signal(barrier, inc=1, device_id=on_line(step), device_id_type=MESH)
    for axis in range(2):
        for step in (1, 2, 3):
            pl.semaphore_signal(barrier, inc=1, device_id=beside(KEYS, axis, step), device_id_type=MESH)

    for h in range(HEADS):
        cols = slice(h * D, (h + 1) * D)
        mine[h, KEYS] = unit(k_ref[:, cols].astype(F32))[0].astype(BF16)
        mine[h, VALUES] = v_ref[:, cols]
    totals[...] = jnp.zeros_like(totals)
    weighted[...] = jnp.zeros_like(weighted)
    dq_t[...] = jnp.zeros_like(dq_t)
    pl.semaphore_wait(barrier, LINE - 1 + 6)

    for step in FAR_FIRST:
        target = on_line(step)
        pltpu.make_async_remote_copy(
            src_ref=mine.at[target[1]],
            dst_ref=kv.at[0, :, pl.ds((LINE - step) * 16, 16), :],
            send_sem=z_sem.at[0],
            recv_sem=z_sem.at[1],
            device_id=target,
            device_id_type=MESH,
        ).start()
    kv[0, :, 0:16, :] = mine[tp]

    q_load.wait()
    do_load.wait()
    for h in range(HEADS):
        cols = slice(h * D, (h + 1) * D)
        cast = unit(q_ref[:, cols].astype(F32))[0].astype(BF16)
        q_n[cols, :] = cast
        q_t[:, cols] = cast.T
        do_n[cols, :] = do_ref[:, cols]
        do_t[:, cols] = do_ref[:, cols].T

    others = kv.at[0, :, 16:BLOCK, :]
    take(others, z_sem.at[1])

    def forward(a, b, axis, step, half=None):
        for kind in range(2):
            src = place(kind, a, b)
            to = ((a - step) % 4, b) if axis == 0 else (a, (b - step) % 4)
            pltpu.make_async_remote_copy(
                src_ref=kv.at[src, kind, rows_of(half), :],
                dst_ref=kv.at[place(kind, *to), kind, rows_of(half), :],
                send_sem=send,
                recv_sem=recv.at[to],
                device_id=beside(kind, axis, step % 4),
                device_id_type=MESH,
            ).start()

    def straight(a):
        return G_SECOND >> a & 1

    def out_second(a):
        for step in (1, -1) + ((2,) if straight(a) else ()):
            forward(a, 0, 1, step)

    def got(a, b):
        take(kv.at[0], recv.at[a, b])
        if b in (1, 3) and not straight(a):
            forward(a, b, 1, b - 2, half=1 if b == 1 else 0)
        if b == 0 and a in (1, 3) and not G_FIRST:
            forward(a, 0, 0, a - 2, half=1 if a == 1 else 0)

    def run(body, group):
        lax.fori_loop(*GROUPS[group], body, 0)

    def pass_1(n, carry):
        scores = jnp.dot(kv[n, KEYS], q_t[...], preferred_element_type=F32)
        value_dots = jnp.dot(kv[n, VALUES], do_t[...], preferred_element_type=F32)
        e = jnp.exp2(scores * EXP2)
        raised[n] = e
        dots[n] = value_dots
        totals[...] += jnp.sum(e.reshape(BLOCK // 8, 8, ROWS), axis=0)
        weighted[...] += jnp.sum((e * value_dots).reshape(BLOCK // 8, 8, ROWS), axis=0)
        return carry

    for step in (1, -1) + ((2,) if G_FIRST else ()):
        forward(0, 0, 0, step)
    out_second(0)
    run(pass_1, 0)
    got(1, 0)
    got(3, 0)
    out_second(1)
    out_second(3)
    if G_FIRST:
        got(2, 0)
        out_second(2)
    got(0, 1)
    got(0, 3)
    run(pass_1, 1)
    if not G_FIRST:
        got(2, 0)
        out_second(2)
    for a in (1, 3):
        got(a, 1)
        got(a, 3)
    run(pass_1, 2)
    got(0, 2)
    got(2, 1)
    got(2, 3)
    run(pass_1, 3)
    got(1, 2)
    got(3, 2)
    run(pass_1, 4)
    got(2, 2)
    run(pass_1, 5)

    total = jnp.sum(totals[...], axis=0, keepdims=True)
    inverse = 1.0 / total
    rows[0:1, :] = inverse
    rows[1:2, :] = jnp.sum(weighted[...], axis=0, keepdims=True) * inverse

    def pass_2(n, carry):
        attend = raised[n] * rows[0:1, :]
        score_grad = (attend * (dots[n] - rows[1:2, :])).astype(BF16)
        part[n, VALUES] = jnp.dot(attend.astype(BF16), do_n[...], preferred_element_type=F32).astype(BF16)
        part[n, KEYS] = (jnp.dot(score_grad, q_n[...], preferred_element_type=F32) * INV).astype(BF16)
        dq_t[...] += jnp.dot(kv[n, KEYS].T, score_grad, preferred_element_type=F32)
        return carry

    def give(src, dst, sem, kind, axis, step):
        pltpu.make_async_remote_copy(
            src_ref=src,
            dst_ref=dst,
            send_sem=r_send,
            recv_sem=sem,
            device_id=beside(kind, axis, step % 4),
            device_id_type=MESH,
        ).start()

    def add(kind, at, half, *refs):
        where = (at, kind, rows_of(half), slice(None))
        value = part[where].astype(F32)
        for ref in refs:
            value = value + ref[...].astype(F32)
        part[where] = value.astype(BF16)

    def buffers(a, axis):
        if axis == 1:
            return (piece_in.at[a], p_recv.at[a], full_in.at[a], f_recv.at[a], R_SECOND >> a & 1)
        return (last_piece, l_recv, last_full, l_recv.at[2], R_FIRST)

    def far(a, b, axis):
        pieces, p_sems, fulls, f_sem, direct = buffers(a, axis)
        for kind in range(2):
            at = place(kind, a, b)
            if direct:
                give(part.at[at, kind], fulls.at[kind, 2], f_sem, kind, axis, 2)
                continue
            for half, step in ((0, 1), (1, -1)):
                give(part.at[at, kind, rows_of(half), :], pieces.at[kind, half], p_sems.at[half], kind, axis, step)

    def near(a, b, axis):
        pieces, p_sems, fulls, f_sem, direct = buffers(a, axis)
        step = 2 - (a if axis == 0 else b)
        half = 0 if step == 1 else 1
        if not direct:
            take(kv.at[0, 0], p_sems.at[half])
        for kind in range(2):
            at = place(kind, a, b)
            if not direct:
                add(kind, at, half, pieces.at[kind, half])
            give(part.at[at, kind], fulls.at[kind, half], f_sem, kind, axis, step)

    def own(a, axis):
        pieces, p_sems, fulls, f_sem, direct = buffers(a, axis)
        sides = 3 if direct else 2
        take(kv.at[0:sides], f_sem)
        for kind in range(2):
            add(kind, place(kind, a, 0), None, *[fulls.at[kind, side] for side in range(sides)])

    run(pass_2, 5)
    far(2, 2, 1)
    run(pass_2, 4)
    far(1, 2, 1)
    far(3, 2, 1)
    near(2, 1, 1)
    near(2, 3, 1)
    run(pass_2, 3)
    far(0, 2, 1)
    run(pass_2, 2)
    for a in (1, 3):
        for b in (1, 3):
            near(a, b, 1)
    own(2, 1)
    far(2, 0, 0)
    run(pass_2, 1)
    near(0, 1, 1)
    near(0, 3, 1)
    run(pass_2, 0)
    for a in (1, 3):
        own(a, 1)
        near(a, 0, 0)

    for h in range(HEADS):
        cols = slice(h * D, (h + 1) * D)
        unit_rows, scale = unit(q_ref[:, cols].astype(F32))
        gq_ref[:, cols] = unit_back(dq_t[:, cols].T * INV, unit_rows, scale).astype(BF16)

    own(0, 1)
    own(0, 0)

    for step in FAR_FIRST:
        pltpu.make_async_remote_copy(
            src_ref=part.at[0, :, pl.ds(step * 16, 16), :],
            dst_ref=line_in.at[me],
            send_sem=y_sem.at[0],
            recv_sem=y_sem.at[1],
            device_id=on_line(step),
            device_id_type=MESH,
        ).start()
    line_in[me] = part[0, :, 0:16, :]
    take(others, z_sem.at[0])
    take(kv.at[0:15], send)
    take(part.at[0:15], r_send)
    take(line_in.at[0 : LINE - 1], y_sem.at[1])
    for h in range(HEADS):
        cols = slice(h * D, (h + 1) * D)
        sums = line_in[h].astype(F32) + line_in[h + 8].astype(F32)
        unit_rows, scale = unit(k_ref[:, cols].astype(F32))
        gk_ref[:, cols] = unit_back(sums[KEYS], unit_rows, scale).astype(BF16)
        gv_ref[:, cols] = sums[VALUES].astype(BF16)
    take(line_in.at[0 : LINE - 1], y_sem.at[0])


def hand_over(*refs):
    for source, target in zip(refs[:3], refs[3:]):
        target[...] = source[...]


def shards(query_raw, key_raw, values, grad_out):
    vmem = pl.BlockSpec(memory_space=pltpu.VMEM)
    anywhere = pl.BlockSpec(memory_space=pl.ANY)
    dma = pltpu.SemaphoreType.DMA
    outs = [jax.ShapeDtypeStruct(a.shape, BF16) for a in (query_raw, key_raw, values)]
    grads = pl.pallas_call(
        kernel,
        out_shape=outs,
        in_specs=[anywhere, vmem, vmem, anywhere],
        out_specs=[vmem] * 3,
        scratch_shapes=[
            pltpu.VMEM((D, ROWS), BF16),
            pltpu.VMEM((D, ROWS), BF16),
            pltpu.VMEM((D, ROWS), BF16),
            pltpu.VMEM((D, ROWS), BF16),
            pltpu.VMEM((ROWS, D), BF16),
            pltpu.VMEM((ROWS, D), BF16),
            pltpu.VMEM((16, BLOCK, ROWS), F32),
            pltpu.VMEM((16, BLOCK, ROWS), F32),
            pltpu.VMEM((8, ROWS), F32),
            pltpu.VMEM((8, ROWS), F32),
            pltpu.VMEM((8, ROWS), F32),
            pltpu.VMEM((D, ROWS), F32),
            pltpu.VMEM((HEADS, 2, 16, D), BF16),
            pltpu.VMEM((16, 2, BLOCK, D), BF16),
            pltpu.VMEM((16, 2, BLOCK, D), BF16),
            pltpu.VMEM((4, 2, 2, HALF, D), BF16),
            pltpu.VMEM((4, 2, 3, BLOCK, D), BF16),
            pltpu.VMEM((2, 2, HALF, D), BF16),
            pltpu.VMEM((2, 3, BLOCK, D), BF16),
            pltpu.VMEM((LINE, 2, 16, D), BF16),
            dma((2,)),
            dma((2,)),
            dma((2,)),
            dma,
            dma((4, 4)),
            dma,
            dma((4, 2)),
            dma((4,)),
            dma((3,)),
        ],
        compiler_params=pltpu.CompilerParams(
            collective_id=0, has_side_effects=True, vmem_limit_bytes=56 * 2**20
        ),
    )(query_raw, key_raw, values, grad_out)
    return pl.pallas_call(hand_over, out_shape=outs, in_specs=[vmem] * 3, out_specs=[vmem] * 3)(*grads)


def solution(mesh):
    split = (P("ctx", "tp"), P(("ctx", "tp"), None), P(("ctx", "tp"), None), P("ctx", "tp"))
    return jax.shard_map(
        shards, mesh=mesh, in_specs=split, out_specs=split[:3], check_vma=False
    )
```

time: 64.5 us -> 59.4 us (0.921)
  local copies, waits for them, and re-layouts: 3.06 us -> 0 us
  Pallas kernels: 60.6 us -> 58.6 us
    unnamed x7 -> x0, local copies, waits for them, and re-layouts: 3.06 us -> none
    pallas_call x1 -> x2, Pallas kernels: 60.6 us -> 58.6 us  [the longest x1 56.9 us: shards(): pl.pallas_call(kernel, out_shape=outs, in_specs=[anywhere, vmem, vmem, an...]
where the time goes in v2:
time: 59.4 us; the launch traced here: 59.2 us
  Pallas kernels  58.6 us (99%)
  between operations  0.64 us (1%)
    pallas_call x1, Pallas kernels, shards(): pl.pallas_call(kernel, out_shape=outs, in_specs=[anywhere, vmem, vmem, an...  56.9 us
    pallas_call x1, Pallas kernels, shards(): pl.pallas_call(hand_over, out_shape=outs, in_specs=[vmem] * 3, out_specs=...  1.7 us

profile of v2, /device:TPU:1, one launch (start us, length us, event | category | flops | bytes accessed | tf_op | source)
XLA Modules:
  0.0 59.2 jit_solution(9088092777680464031)
XLA Ops:
  0.6 56.9 %shard_map.67 = (bf16[128,1024]{1,0:T(8,128)(2,1)}, bf16[16,1024]{1,0:T(8,128)(2,1)}, bf16[16,1024]{1,0:T(8,128)(2,1)}) custom-call(bf16[128,1024]{1,0:T(8,128)(2,1)} %q_in.1, bf16[16,1024]{1,0:T(8,128)(2,1)} %k_ref.1, bf16[16,1024]{1,0:T(8,128)(2,1)} %v_ref.1, bf16[128,1024]{1,0:T(8,128)(2,1)} %do_in.1), custom_call_target="tpu_custom_call" | custom-call | tf_op jit(solution)/shard_map/pallas_call | solution.py:328
  57.5 1.7 %shard_map.68 = (bf16[128,1024]{1,0:T(8,128)(2,1)}, bf16[16,1024]{1,0:T(8,128)(2,1)}, bf16[16,1024]{1,0:T(8,128)(2,1)}) custom-call(bf16[128,1024]{1,0:T(8,128)(2,1)} %get-tuple-element.6.refs_0_, bf16[16,1024]{1,0:T(8,128)(2,1)} %get-tuple-element.7.refs_1_, bf16[16,1024]{1,0:T(8,128)(2,1)} %get-tuple-element.8.refs_2_), custom_call_target="tpu_custom_call" | custom-call | tf_op jit(solution)/shard_map/pallas_call | solution.py:368

commit v3 on v2

--- a/solution.py
+++ b/solution.py
@@ -58,9 +58,9 @@
 
 
 def kernel(
-    q_in, k_ref, v_ref, do_in,
+    q_in, k_in, v_in, do_in,
     gq_ref, gk_ref, gv_ref,
-    q_ref, do_ref, q_t, do_t, q_n, do_n, raised, dots, totals, weighted, rows, dq_t,
+    q_ref, k_ref, v_ref, do_ref, q_t, do_t, q_n, do_n, raised, dots, totals, weighted, rows, dq_t,
     mine, kv, part, piece_in, full_in, last_piece, last_full, line_in,
     load, z_sem, y_sem, send, recv, r_send, p_recv, f_recv, l_recv,
 ):
@@ -81,10 +81,6 @@
     def take(ref, sem):
         pltpu.make_async_copy(ref, ref, sem).wait()
 
-    q_load = pltpu.make_async_copy(q_in, q_ref, load.at[0])
-    do_load = pltpu.make_async_copy(do_in, do_ref, load.at[1])
-    q_load.start()
-    do_load.start()
     barrier = pltpu.get_barrier_semaphore()
     for step in FAR_FIRST:
         pl.semaphore_signal(barrier, inc=1, device_id=on_line(step), device_id_type=MESH)
@@ -92,13 +88,21 @@
         for step in (1, 2, 3):
             pl.semaphore_signal(barrier, inc=1, device_id=beside(KEYS, axis, step), device_id_type=MESH)
 
+    loads = [
+        pltpu.make_async_copy(source, target, load.at[n])
+        for n, (source, target) in enumerate(((k_in, k_ref), (v_in, v_ref), (q_in, q_ref), (do_in, do_ref)))
+    ]
+    for copy in loads:
+        copy.start()
+    totals[...] = jnp.zeros_like(totals)
+    weighted[...] = jnp.zeros_like(weighted)
+    dq_t[...] = jnp.zeros_like(dq_t)
+    loads[0].wait()
+    loads[1].wait()
     for h in range(HEADS):
         cols = slice(h * D, (h + 1) * D)
         mine[h, KEYS] = unit(k_ref[:, cols].astype(F32))[0].astype(BF16)
         mine[h, VALUES] = v_ref[:, cols]
-    totals[...] = jnp.zeros_like(totals)
-    weighted[...] = jnp.zeros_like(weighted)
-    dq_t[...] = jnp.zeros_like(dq_t)
     pl.semaphore_wait(barrier, LINE - 1 + 6)
 
     for step in FAR_FIRST:
@@ -113,8 +117,8 @@
         ).start()
     kv[0, :, 0:16, :] = mine[tp]
 
-    q_load.wait()
-    do_load.wait()
+    loads[2].wait()
+    loads[3].wait()
     for h in range(HEADS):
         cols = slice(h * D, (h + 1) * D)
         cast = unit(q_ref[:, cols].astype(F32))[0].astype(BF16)
@@ -169,34 +173,36 @@
     for step in (1, -1) + ((2,) if G_FIRST else ()):
         forward(0, 0, 0, step)
     out_second(0)
+    def block(body, *at):
+        for one in at:
+            n = PLACE[one]
+            lax.fori_loop(n, n + 1, body, 0)
+
     run(pass_1, 0)
     got(1, 0)
+    out_second(1)
     got(3, 0)
-    out_second(1)
     out_second(3)
-    if G_FIRST:
-        got(2, 0)
-        out_second(2)
+    got(2, 0)
+    out_second(2)
     got(0, 1)
     got(0, 3)
     run(pass_1, 1)
-    if not G_FIRST:
-        got(2, 0)
-        out_second(2)
-    for a in (1, 3):
-        got(a, 1)
-        got(a, 3)
+    got(1, 1)
+    got(1, 3)
+    got(3, 1)
+    got(3, 3)
     run(pass_1, 2)
     got(0, 2)
     got(2, 1)
     got(2, 3)
     run(pass_1, 3)
     got(1, 2)
+    block(pass_1, (1, 2), (2, 1))
     got(3, 2)
-    run(pass_1, 4)
+    block(pass_1, (3, 2), (2, 3))
     got(2, 2)
     run(pass_1, 5)
-
     total = jnp.sum(totals[...], axis=0, keepdims=True)
     inverse = 1.0 / total
     rows[0:1, :] = inverse
@@ -232,9 +238,9 @@
             return (piece_in.at[a], p_recv.at[a], full_in.at[a], f_recv.at[a], R_SECOND >> a & 1)
         return (last_piece, l_recv, last_full, l_recv.at[2], R_FIRST)
 
-    def far(a, b, axis):
+    def far(a, b, axis, kinds=(KEYS, VALUES)):
         pieces, p_sems, fulls, f_sem, direct = buffers(a, axis)
-        for kind in range(2):
+        for kind in kinds:
             at = place(kind, a, b)
             if direct:
                 give(part.at[at, kind], fulls.at[kind, 2], f_sem, kind, axis, 2)
@@ -261,25 +267,38 @@
         for kind in range(2):
             add(kind, place(kind, a, 0), None, *[fulls.at[kind, side] for side in range(sides)])
 
-    run(pass_2, 5)
+    K1, V1 = (KEYS,), (VALUES,)
+    block(pass_2, (2, 2))
     far(2, 2, 1)
-    run(pass_2, 4)
-    far(1, 2, 1)
-    far(3, 2, 1)
+    block(pass_2, (1, 2))
+    far(1, 2, 1, K1)
+    block(pass_2, (3, 2))
+    far(3, 2, 1, K1)
+    block(pass_2, (2, 1))
+    far(1, 2, 1, V1)
+    block(pass_2, (2, 3))
+    far(3, 2, 1, V1)
+    block(pass_2, (0, 2))
+    far(0, 2, 1, K1)
+    block(pass_2, (2, 0))
+    far(0, 2, 1, V1)
     near(2, 1, 1)
+    block(pass_2, (1, 1))
     near(2, 3, 1)
-    run(pass_2, 3)
-    far(0, 2, 1)
-    run(pass_2, 2)
-    for a in (1, 3):
-        for b in (1, 3):
-            near(a, b, 1)
+    block(pass_2, (1, 3))
+    near(1, 1, 1)
+    block(pass_2, (3, 1))
+    near(1, 3, 1)
+    near(3, 1, 1)
+    block(pass_2, (3, 3))
+    near(3, 3, 1)
+    block(pass_2, (1, 0), (3, 0))
     own(2, 1)
     far(2, 0, 0)
-    run(pass_2, 1)
+    block(pass_2, (0, 1), (0, 3))
     near(0, 1, 1)
     near(0, 3, 1)
-    run(pass_2, 0)
+    block(pass_2, (0, 0))
     for a in (1, 3):
         own(a, 1)
         near(a, 0, 0)
@@ -328,10 +347,12 @@
     grads = pl.pallas_call(
         kernel,
         out_shape=outs,
-        in_specs=[anywhere, vmem, vmem, anywhere],
+        in_specs=[anywhere] * 4,
         out_specs=[vmem] * 3,
         scratch_shapes=[
             pltpu.VMEM((D, ROWS), BF16),
+            pltpu.VMEM((16, ROWS), BF16),
+            pltpu.VMEM((16, ROWS), BF16),
             pltpu.VMEM((D, ROWS), BF16),
             pltpu.VMEM((D, ROWS), BF16),
             pltpu.VMEM((D, ROWS), BF16),
@@ -351,7 +372,7 @@
             pltpu.VMEM((2, 2, HALF, D), BF16),
             pltpu.VMEM((2, 3, BLOCK, D), BF16),
             pltpu.VMEM((LINE, 2, 16, D), BF16),
-            dma((2,)),
+            dma((4,)),
             dma((2,)),
             dma((2,)),
             dma,

time: 59.4 us -> 55.9 us (0.941)
  Pallas kernels: 58.6 us -> 55.1 us
    pallas_call x1, Pallas kernels: 56.9 us -> 53.4 us  [shards(): pl.pallas_call(kernel, out_shape=outs, in_specs=[anywhere] * 4, out_specs...]
where the time goes in v3:
time: 55.9 us; the launch traced here: 55.8 us
  Pallas kernels  55.1 us (99%)
  between operations  0.64 us (1%)
    pallas_call x1, Pallas kernels, shards(): pl.pallas_call(kernel, out_shape=outs, in_specs=[anywhere] * 4, out_specs...  53.4 us
    pallas_call x1, Pallas kernels, shards(): pl.pallas_call(hand_over, out_shape=outs, in_specs=[vmem] * 3, out_specs=...  1.7 us

profile of v3, /device:TPU:1, one launch (start us, length us, event | category | flops | bytes accessed | tf_op | source)
XLA Modules:
  0.0 55.8 jit_solution(441820905977756796)
XLA Ops:
  0.6 53.4 %shard_map.67 = (bf16[128,1024]{1,0:T(8,128)(2,1)}, bf16[16,1024]{1,0:T(8,128)(2,1)}, bf16[16,1024]{1,0:T(8,128)(2,1)}) custom-call(bf16[128,1024]{1,0:T(8,128)(2,1)} %q_in.1, bf16[16,1024]{1,0:T(8,128)(2,1)} %k_in.1, bf16[16,1024]{1,0:T(8,128)(2,1)} %v_in.1, bf16[128,1024]{1,0:T(8,128)(2,1)} %do_in.1), custom_call_target="tpu_custom_call" | custom-call | tf_op jit(solution)/shard_map/pallas_call | solution.py:347
  54.1 1.7 %shard_map.68 = (bf16[128,1024]{1,0:T(8,128)(2,1)}, bf16[16,1024]{1,0:T(8,128)(2,1)}, bf16[16,1024]{1,0:T(8,128)(2,1)}) custom-call(bf16[128,1024]{1,0:T(8,128)(2,1)} %get-tuple-element.6.refs_0_, bf16[16,1024]{1,0:T(8,128)(2,1)} %get-tuple-element.7.refs_1_, bf16[16,1024]{1,0:T(8,128)(2,1)} %get-tuple-element.8.refs_2_), custom_call_target="tpu_custom_call" | custom-call | tf_op jit(solution)/shard_map/pallas_call | solution.py:389

commit v4 on v3

--- a/solution.py
+++ b/solution.py
@@ -346,7 +346,7 @@
     outs = [jax.ShapeDtypeStruct(a.shape, BF16) for a in (query_raw, key_raw, values)]
     grads = pl.pallas_call(
         kernel,
-        out_shape=outs,
+        out_shape=[pltpu.VMEM(a.shape, a.dtype) for a in outs],
         in_specs=[anywhere] * 4,
         out_specs=[vmem] * 3,
         scratch_shapes=[
@@ -386,7 +386,9 @@
             collective_id=0, has_side_effects=True, vmem_limit_bytes=56 * 2**20
         ),
     )(query_raw, key_raw, values, grad_out)
-    return pl.pallas_call(hand_over, out_shape=outs, in_specs=[vmem] * 3, out_specs=[vmem] * 3)(*grads)
+    return pl.pallas_call(hand_over, out_shape=outs, in_specs=[vmem] * 3, out_specs=[vmem] * 3)(
+        *[pltpu.with_memory_space_constraint(grad, pltpu.VMEM) for grad in grads]
+    )
 
 
 def solution(mesh):

time: 55.9 us -> 54.1 us (0.968)
  Pallas kernels: 55.1 us -> 53.4 us
    pallas_call x1, Pallas kernels: 1.7 us -> 0.74 us  [shards(): pl.pallas_call(hand_over, out_shape=outs, in_specs=[vmem] * 3, out_specs=...]
    pallas_call x1, Pallas kernels: 53.4 us -> 52.7 us  [shards(): pl.pallas_call(kernel, out_shape=[pltpu.VMEM(a.shape, a.dtype) for a in o...]
where the time goes in v4:
time: 54.1 us
  Pallas kernels  53.4 us (99%)
  between operations  0.64 us (1%)
    pallas_call x1, Pallas kernels, shards(): pl.pallas_call(kernel, out_shape=[pltpu.VMEM(a.shape, a.dtype) for a in o...  52.7 us

profile of v4, /device:TPU:1, one launch (start us, length us, event | category | flops | bytes accessed | tf_op | source)
XLA Modules:
  0.0 54.1 jit_solution(4614169488428684084)
XLA Ops:
  0.6 52.7 %shard_map.67 = (bf16[128,1024]{1,0:T(8,128)(2,1)S(1)}, bf16[16,1024]{1,0:T(8,128)(2,1)S(1)}, bf16[16,1024]{1,0:T(8,128)(2,1)S(1)}) custom-call(bf16[128,1024]{1,0:T(8,128)(2,1)} %q_in.1, bf16[16,1024]{1,0:T(8,128)(2,1)} %k_in.1, bf16[16,1024]{1,0:T(8,128)(2,1)} %v_in.1, bf16[128,1024]{1,0:T(8,128)(2,1)} %do_in.1), custom_call_target="tpu_custom_call" | custom-call | tf_op jit(solution)/shard_map/pallas_call | solution.py:347
  53.3 0.7 %shard_map.68 = (bf16[128,1024]{1,0:T(8,128)(2,1)}, bf16[16,1024]{1,0:T(8,128)(2,1)}, bf16[16,1024]{1,0:T(8,128)(2,1)}) custom-call(bf16[128,1024]{1,0:T(8,128)(2,1)S(1)} %get-tuple-element.6.refs_0_, bf16[16,1024]{1,0:T(8,128)(2,1)S(1)} %get-tuple-element.7.refs_1_, bf16[16,1024]{1,0:T(8,128)(2,1)S(1)} %get-tuple-element.8.refs_2_), custom_call_target="tpu_custom_call" | custom-call | tf_op jit(solution)/shard_map/pallas_call | solution.py:389

commit v5 on v4

v5 whole, which is shorter than its diff:
```python
import math

import jax
import jax.numpy as jnp
from jax import lax
from jax.experimental import pallas as pl
from jax.experimental.pallas import tpu as pltpu
from jax.sharding import PartitionSpec as P

F32 = jnp.float32
BF16 = jnp.bfloat16
MESH = pl.DeviceIdType.MESH
EPS = 1e-6
D = 128
HEADS = 8
ROWS = 1024
BLOCK = 256
LINE = 16
INV = 1.0 / math.sqrt(D)
EXP2 = INV * math.log2(math.e)
KEYS, VALUES = 0, 1

BLOCKS = ((0, 0), (0, 3), (0, 1), (0, 2), (1, 0), (1, 3), (1, 1), (1, 2))
PLACE = {at: n for n, at in enumerate(BLOCKS)}
LINES = [(1, dz) for dz in (4, 3, 5, 2, 6, 1, 7, 0)] + [(0, dz) for dz in (4, 3, 5, 2, 6, 1, 7)]
LATE = 1


def unit(raw):
    scale = lax.rsqrt(jnp.mean(raw * raw, axis=-1, keepdims=True) + EPS)
    return raw * scale, scale


def unit_back(grad, unit_rows, scale):
    return scale * (grad - unit_rows * jnp.mean(grad * unit_rows, axis=-1, keepdims=True))


def kernel(
    q_in, k_in, v_in, do_in,
    gq_ref, gk_ref, gv_ref,
    q_ref, k_ref, v_ref, do_ref, q_t, do_t, q_n, do_n, raised, dots, totals, weighted, rows, dq_t,
    mine, kv, part, sib_in, y_in, x_in, line_in, gq_out, gq_in,
    load, swap, z_sem, l_sem, send, recv, s_send, s_recv, t_send, t_recv, r_send, yr_recv, xr_recv, back,
):
    ctx = lax.axis_index("ctx")
    tp = lax.axis_index("tp")
    y, x = ctx // 8, ctx % 4
    z = ((ctx // 4) % 2) * 4 + tp // 2
    core = tp % 2
    group = x // 2
    stays = core == group
    def device(at_x, at_y, at_z, at_core):
        at_z = at_z % 8
        return ((at_y % 4) * 8 + (at_z // 4) * 4 + at_x % 4, (at_z % 4) * 2 + at_core)

    beside_x = device(x + 1 - 2 * (x % 2), y, z, core)
    sibling = device(x, y, z, 1 - core)
    partner = device(x + 2, y, z, 1 - core)

    def beside_y(step):
        return device(x, y + step + 4, z, core)

    def on_line(l, dz):
        return device(x + 2 * l, y, z + dz, core)

    def copy_to(src, dst, send_sem, recv_sem, target):
        pltpu.make_async_remote_copy(
            src_ref=src, dst_ref=dst, send_sem=send_sem, recv_sem=recv_sem, device_id=target, device_id_type=MESH
        ).start()

    def take(ref, sem):
        pltpu.make_async_copy(ref, ref, sem).wait()

    barrier = pltpu.get_barrier_semaphore()
    greeted = [on_line(l, dz) for l, dz in LINES] + [beside_y(step) for step in (1, 2, 3)]
    greeted += [beside_x, sibling, partner]
    for target in greeted:
        pl.semaphore_signal(barrier, inc=1, device_id=target, device_id_type=MESH)
    k_load = pltpu.make_async_copy(k_in, k_ref, load.at[0])
    v_load = pltpu.make_async_copy(v_in, v_ref, load.at[1])
    k_load.start()
    v_load.start()

    @pl.when(stays)
    def _():
        pltpu.make_async_copy(q_in, q_ref, swap.at[1]).start()
        pltpu.make_async_copy(do_in, do_ref, swap.at[2]).start()

    totals[...] = jnp.zeros_like(totals)
    weighted[...] = jnp.zeros_like(weighted)
    dq_t[...] = jnp.zeros_like(dq_t)
    k_load.wait()
    v_load.wait()
    for h in range(HEADS):
        cols = slice(h * D, (h + 1) * D)
        mine[h, KEYS] = unit(k_ref[:, cols].astype(F32))[0].astype(BF16)
        mine[h, VALUES] = v_ref[:, cols]
    pl.semaphore_wait(barrier, len(greeted))

    for l, dz in LINES:
        head = 2 * ((z + dz) % 4) + ((x + 2 * l) % 4) // 2
        spot = (l * 8 + (8 - dz) % 8) * 16
        copy_to(mine.at[head], kv.at[0, :, spot : spot + 16, :], z_sem.at[0], z_sem.at[1], on_line(l, dz))
    kv[0, :, 0:16, :] = mine[2 * (z % 4) + group]

    @pl.when(jnp.logical_not(stays))
    def _():
        copy_to(q_in, q_ref, swap.at[0], swap.at[1], partner)
        copy_to(do_in, do_ref, swap.at[3], swap.at[2], partner)

    others = kv.at[0, :, 16:BLOCK, :]
    take(others, z_sem.at[1])

    def along_x(kind, i, b):
        to = PLACE[1 - i, b]
        copy_to(kv.at[2 * PLACE[i, b], kind], kv.at[2 * to, kind], send, recv.at[kind, to], beside_x)

    def along_y(kind, i, b):
        for step in (1, 3, 2):
            to = PLACE[i, (b - step) % 4]
            copy_to(kv.at[2 * PLACE[i, b], kind], kv.at[2 * to, kind], send, recv.at[kind, to], beside_y(step))

    def got(kind, i, b):
        n = PLACE[i, b]
        take(kv.at[0, 0], recv.at[kind, n])
        if kind == KEYS and b == 0:
            along_y(kind, i, b)
        if kind == VALUES and i == 0:
            along_x(kind, i, b)
        copy_to(kv.at[2 * n, kind], kv.at[2 * n + 1, kind], s_send, s_recv.at[n], sibling)

    along_x(KEYS, 0, 0)
    along_y(VALUES, 0, 0)
    along_y(KEYS, 0, 0)
    along_x(VALUES, 0, 0)
    copy_to(kv.at[0], kv.at[1], s_send, s_recv.at[0], sibling)

    def pass_1(n, carry):
        scores = jnp.dot(kv[n, KEYS], q_t[...], preferred_element_type=F32)
        value_dots = jnp.dot(kv[n, VALUES], do_t[...], preferred_element_type=F32)
        e = jnp.exp2(scores * EXP2)
        raised[n] = e
        dots[n] = value_dots
        totals[...] += jnp.sum(e.reshape(BLOCK // 8, 8, ROWS), axis=0)
        weighted[...] += jnp.sum((e * value_dots).reshape(BLOCK // 8, 8, ROWS), axis=0)
        return carry

    def run(body, low, high):
        lax.fori_loop(low, high, body, 0, unroll=True)

    def shared(i, b):
        take(kv.at[0], s_recv.at[PLACE[i, b]])

    take(q_ref, swap.at[1])
    for h in range(HEADS):
        cols = slice(h * D, (h + 1) * D)
        cast = unit(q_ref[:, cols].astype(F32))[0].astype(BF16)
        q_n[cols, :] = cast
        q_t[:, cols] = cast.T
    got(KEYS, 1, 0)
    for b in (3, 1, 2):
        got(VALUES, 0, b)
    take(do_ref, swap.at[2])
    for h in range(HEADS):
        cols = slice(h * D, (h + 1) * D)
        do_n[cols, :] = do_ref[:, cols]
        do_t[:, cols] = do_ref[:, cols].T
    def fetch(m):
        i, b = BLOCKS[m]
        if (i, b) != (1, 0):
            got(KEYS, i, b)
        if i:
            got(VALUES, i, b)

    run(pass_1, 0, 1)
    fetch(1)
    for m in range(1, 8):
        if m < 7:
            fetch(m + 1)
        shared(*BLOCKS[m - 1])
        run(pass_1, 2 * m - 1, 2 * m + 1)
    shared(*BLOCKS[7])
    run(pass_1, 15, 16)
    total = jnp.sum(totals[...], axis=0, keepdims=True)
    inverse = 1.0 / total
    rows[0:1, :] = inverse
    rows[1:2, :] = jnp.sum(weighted[...], axis=0, keepdims=True) * inverse

    def pass_2(t, carry):
        n = 15 - t
        attend = raised[n] * rows[0:1, :]
        score_grad = (attend * (dots[n] - rows[1:2, :])).astype(BF16)
        part[n, VALUES] = jnp.dot(attend.astype(BF16), do_n[...], preferred_element_type=F32).astype(BF16)
        part[n, KEYS] = (jnp.dot(score_grad, q_n[...], preferred_element_type=F32) * INV).astype(BF16)
        dq_t[...] += jnp.dot(kv[n, KEYS].T, score_grad, preferred_element_type=F32)
        return carry

    def share(m):
        copy_to(part.at[2 * m + 1], sib_in.at[m], t_send, t_recv.at[m], sibling)

    def add(i, b, kind, *refs):
        n = 2 * PLACE[i, b]
        value = part[n, kind].astype(F32)
        for ref in refs:
            value = value + ref[...].astype(F32)
        part[n, kind] = value.astype(BF16)

    def settle(i, b):
        m = PLACE[i, b]
        take(kv.at[0], t_recv.at[m])
        came = [sib_in.at[m, VALUES]]
        if i == 0:
            take(kv.at[0, 0], xr_recv.at[b])
            came.append(x_in.at[b])
        add(i, b, VALUES, *came)
        if i == 1:
            copy_to(part.at[2 * m, VALUES], x_in.at[b], r_send, xr_recv.at[b], beside_x)
        elif b:
            copy_to(part.at[2 * m, VALUES], y_in.at[2, b - 1], r_send, yr_recv.at[2], beside_y(b))
        add(i, b, KEYS, sib_in.at[m, KEYS])
        if b:
            copy_to(part.at[2 * m, KEYS], y_in.at[i, b - 1], r_send, yr_recv.at[i], beside_y(b))

    def gather_y(which, i, kind, *more):
        take(y_in.at[0], yr_recv.at[which])
        add(i, 0, kind, y_in.at[which, 0], y_in.at[which, 1], y_in.at[which, 2], *more)

    run(pass_2, 0, 1)
    share(7)
    for m in range(6, -1, -1):
        run(pass_2, 13 - 2 * m, 15 - 2 * m)
        share(m)
        settle(*BLOCKS[m + 1])
        if m == LATE:
            gather_y(1, 1, KEYS)
            copy_to(part.at[2 * PLACE[1, 0], KEYS], x_in.at[4], r_send, xr_recv.at[4], beside_x)
    run(pass_2, 15, 16)

    for h in range(HEADS):
        cols = slice(h * D, (h + 1) * D)
        unit_rows, scale = unit(q_ref[:, cols].astype(F32))
        gq_out[:, cols] = unit_back(dq_t[:, cols].T * INV, unit_rows, scale).astype(BF16)

    @pl.when(jnp.logical_not(stays))
    def _():
        copy_to(gq_out, gq_in, back.at[0], back.at[1], partner)

    settle(0, 0)
    take(kv.at[0, 0], xr_recv.at[4])
    gather_y(0, 0, KEYS, x_in.at[4])
    gather_y(2, 0, VALUES)

    me = group * 8 + z
    for l, dz in LINES:
        spot = (l * 8 + dz) * 16
        copy_to(part.at[0, :, spot : spot + 16, :], line_in.at[me], l_sem.at[0], l_sem.at[1], on_line(l, dz))
    line_in[me] = part[0, :, 0:16, :]
    take(others, z_sem.at[0])
    take(kv.at[0:7], send)
    take(kv.at[0:8], s_send)
    take(part.at[0:8], t_send)
    take(part.at[0:7], r_send)

    @pl.when(stays)
    def _():
        gq_ref[...] = gq_out[...]

    @pl.when(jnp.logical_not(stays))
    def _():
        take(q_ref, swap.at[0])
        take(do_ref, swap.at[3])
        take(gq_out, back.at[0])
        take(gq_in, back.at[1])
        gq_ref[...] = gq_in[...]

    take(line_in.at[0 : LINE - 1], l_sem.at[1])
    for h in range(HEADS):
        cols = slice(h * D, (h + 1) * D)
        low = (h % 2) * 8 + h // 2
        sums = line_in[low].astype(F32) + line_in[low + 4].astype(F32)
        unit_rows, scale = unit(k_ref[:, cols].astype(F32))
        gk_ref[:, cols] = unit_back(sums[KEYS], unit_rows, scale).astype(BF16)
        gv_ref[:, cols] = sums[VALUES].astype(BF16)
    take(line_in.at[0 : LINE - 1], l_sem.at[0])


def hand_over(*refs):
    for source, target in zip(refs[:3], refs[3:]):
        target[...] = source[...]


def shards(query_raw, key_raw, values, grad_out):
    vmem = pl.BlockSpec(memory_space=pltpu.VMEM)
    anywhere = pl.BlockSpec(memory_space=pl.ANY)
    dma = pltpu.SemaphoreType.DMA
    outs = [jax.ShapeDtypeStruct(a.shape, BF16) for a in (query_raw, key_raw, values)]
    grads = pl.pallas_call(
        kernel,
        out_shape=[pltpu.VMEM(a.shape, a.dtype) for a in outs],
        in_specs=[anywhere] * 4,
        out_specs=[vmem] * 3,
        scratch_shapes=[
            pltpu.VMEM((D, ROWS), BF16),
            pltpu.VMEM((16, ROWS), BF16),
            pltpu.VMEM((16, ROWS), BF16),
            pltpu.VMEM((D, ROWS), BF16),
            pltpu.VMEM((D, ROWS), BF16),
            pltpu.VMEM((D, ROWS), BF16),
            pltpu.VMEM((ROWS, D), BF16),
            pltpu.VMEM((ROWS, D), BF16),
            pltpu.VMEM((16, BLOCK, ROWS), F32),
            pltpu.VMEM((16, BLOCK, ROWS), F32),
            pltpu.VMEM((8, ROWS), F32),
            pltpu.VMEM((8, ROWS), F32),
            pltpu.VMEM((8, ROWS), F32),
            pltpu.VMEM((D, ROWS), F32),
            pltpu.VMEM((HEADS, 2, 16, D), BF16),
            pltpu.VMEM((16, 2, BLOCK, D), BF16),
            pltpu.VMEM((16, 2, BLOCK, D), BF16),
            pltpu.VMEM((8, 2, BLOCK, D), BF16),
            pltpu.VMEM((3, 3, BLOCK, D), BF16),
            pltpu.VMEM((5, BLOCK, D), BF16),
            pltpu.VMEM((LINE, 2, 16, D), BF16),
            pltpu.VMEM((D, ROWS), BF16),
            pltpu.VMEM((D, ROWS), BF16),
            dma((2,)),
            dma((4,)),
            dma((2,)),
            dma((2,)),
            dma,
            dma((2, 8)),
            dma,
            dma((8,)),
            dma,
            dma((8,)),
            dma,
            dma((3,)),
            dma((5,)),
            dma((2,)),
        ],
        compiler_params=pltpu.CompilerParams(
            collective_id=0, has_side_effects=True, vmem_limit_bytes=56 * 2**20
        ),
    )(query_raw, key_raw, values, grad_out)
    return pl.pallas_call(hand_over, out_shape=outs, in_specs=[vmem] * 3, out_specs=[vmem] * 3)(
        *[pltpu.with_memory_space_constraint(grad, pltpu.VMEM) for grad in grads]
    )


def solution(mesh):
    split = (P("ctx", "tp"), P(("ctx", "tp"), None), P(("ctx", "tp"), None), P("ctx", "tp"))
    return jax.shard_map(
        shards, mesh=mesh, in_specs=split, out_specs=split[:3], check_vma=False
    )
```

time: 54.1 us -> 52.1 us (0.963)
  Pallas kernels: 53.4 us -> 51.3 us
    pallas_call x1, Pallas kernels: 52.7 us -> 50.6 us  [shards(): pl.pallas_call(kernel, out_shape=[pltpu.VMEM(a.shape, a.dtype) for a in o...]
where the time goes in v5:
time: 52.1 us; the launch traced here: 52 us
  Pallas kernels  51.3 us (98%)
  between operations  0.64 us (1%)
    pallas_call x1, Pallas kernels, shards(): pl.pallas_call(kernel, out_shape=[pltpu.VMEM(a.shape, a.dtype) for a in o...  50.6 us

profile of v5, /device:TPU:1, one launch (start us, length us, event | category | flops | bytes accessed | tf_op | source)
XLA Modules:
  0.0 52.0 jit_solution(12083784811769709537)
XLA Ops:
  0.6 50.6 %shard_map.67 = (bf16[128,1024]{1,0:T(8,128)(2,1)S(1)}, bf16[16,1024]{1,0:T(8,128)(2,1)S(1)}, bf16[16,1024]{1,0:T(8,128)(2,1)S(1)}) custom-call(bf16[128,1024]{1,0:T(8,128)(2,1)} %q_in.1, bf16[16,1024]{1,0:T(8,128)(2,1)} %k_in.1, bf16[16,1024]{1,0:T(8,128)(2,1)} %v_in.1, bf16[128,1024]{1,0:T(8,128)(2,1)} %do_in.1), custom_call_target="tpu_custom_call" | custom-call | tf_op jit(solution)/shard_map/pallas_call | solution.py:297
  51.2 0.7 %shard_map.68 = (bf16[128,1024]{1,0:T(8,128)(2,1)}, bf16[16,1024]{1,0:T(8,128)(2,1)}, bf16[16,1024]{1,0:T(8,128)(2,1)}) custom-call(bf16[128,1024]{1,0:T(8,128)(2,1)S(1)} %get-tuple-element.6.refs_0_, bf16[16,1024]{1,0:T(8,128)(2,1)S(1)} %get-tuple-element.7.refs_1_, bf16[16,1024]{1,0:T(8,128)(2,1)S(1)} %get-tuple-element.8.refs_2_), custom_call_target="tpu_custom_call" | custom-call | tf_op jit(solution)/shard_map/pallas_call | solution.py:345

commit v6 on v5

--- a/solution.py
+++ b/solution.py
@@ -20,12 +20,10 @@
 EXP2 = INV * math.log2(math.e)
 KEYS, VALUES = 0, 1
 
+
 BLOCKS = ((0, 0), (0, 3), (0, 1), (0, 2), (1, 0), (1, 3), (1, 1), (1, 2))
 PLACE = {at: n for n, at in enumerate(BLOCKS)}
 LINES = [(1, dz) for dz in (4, 3, 5, 2, 6, 1, 7, 0)] + [(0, dz) for dz in (4, 3, 5, 2, 6, 1, 7)]
-LATE = 1
-
-
 def unit(raw):
     scale = lax.rsqrt(jnp.mean(raw * raw, axis=-1, keepdims=True) + EPS)
     return raw * scale, scale
@@ -38,8 +36,8 @@
 def kernel(
     q_in, k_in, v_in, do_in,
     gq_ref, gk_ref, gv_ref,
-    q_ref, k_ref, v_ref, do_ref, q_t, do_t, q_n, do_n, raised, dots, totals, weighted, rows, dq_t,
-    mine, kv, part, sib_in, y_in, x_in, line_in, gq_out, gq_in,
+    q_ref, k_ref, v_ref, do_ref, q_t, do_t, q_n, do_n, raised, dots, grads, totals, weighted, rows, dq_t,
+    k_unit, k_scale, mine, kv, part, sib_in, y_in, x_in, line_in, gq_out, gq_in,
     load, swap, z_sem, l_sem, send, recv, s_send, s_recv, t_send, t_recv, r_send, yr_recv, xr_recv, back,
 ):
     ctx = lax.axis_index("ctx")
@@ -93,7 +91,9 @@
     v_load.wait()
     for h in range(HEADS):
         cols = slice(h * D, (h + 1) * D)
-        mine[h, KEYS] = unit(k_ref[:, cols].astype(F32))[0].astype(BF16)
+        k_unit[h], scale = unit(k_ref[:, cols].astype(F32))
+        k_scale[h] = jnp.broadcast_to(scale, (16, D))
+        mine[h, KEYS] = k_unit[h].astype(BF16)
         mine[h, VALUES] = v_ref[:, cols]
     pl.semaphore_wait(barrier, len(greeted))
 
@@ -111,14 +111,14 @@
     others = kv.at[0, :, 16:BLOCK, :]
     take(others, z_sem.at[1])
 
-    def along_x(kind, i, b):
+    def along_x(kind, i, b, part_of=slice(0, BLOCK)):
         to = PLACE[1 - i, b]
-        copy_to(kv.at[2 * PLACE[i, b], kind], kv.at[2 * to, kind], send, recv.at[kind, to], beside_x)
-
-    def along_y(kind, i, b):
+        copy_to(kv.at[2 * PLACE[i, b], kind, part_of], kv.at[2 * to, kind, part_of], send, recv.at[kind, to], beside_x)
+
+    def along_y(kind, i, b, part_of=slice(0, BLOCK)):
         for step in (1, 3, 2):
             to = PLACE[i, (b - step) % 4]
-            copy_to(kv.at[2 * PLACE[i, b], kind], kv.at[2 * to, kind], send, recv.at[kind, to], beside_y(step))
+            copy_to(kv.at[2 * PLACE[i, b], kind, part_of], kv.at[2 * to, kind, part_of], send, recv.at[kind, to], beside_y(step))
 
     def got(kind, i, b):
         n = PLACE[i, b]
@@ -135,18 +135,18 @@
     along_x(VALUES, 0, 0)
     copy_to(kv.at[0], kv.at[1], s_send, s_recv.at[0], sibling)
 
-    def pass_1(n, carry):
-        scores = jnp.dot(kv[n, KEYS], q_t[...], preferred_element_type=F32)
-        value_dots = jnp.dot(kv[n, VALUES], do_t[...], preferred_element_type=F32)
+    def pass_1(low, high):
+        count = (high - low) * BLOCK
+        scores = jnp.dot(kv[low:high, KEYS].reshape(count, D), q_t[...], preferred_element_type=F32)
+        value_dots = jnp.dot(kv[low:high, VALUES].reshape(count, D), do_t[...], preferred_element_type=F32)
         e = jnp.exp2(scores * EXP2)
-        raised[n] = e
-        dots[n] = value_dots
-        totals[...] += jnp.sum(e.reshape(BLOCK // 8, 8, ROWS), axis=0)
-        weighted[...] += jnp.sum((e * value_dots).reshape(BLOCK // 8, 8, ROWS), axis=0)
-        return carry
+        raised[low:high] = e.reshape(high - low, BLOCK, ROWS)
+        dots[low:high] = value_dots.reshape(high - low, BLOCK, ROWS)
+        totals[...] += jnp.sum(e.reshape(count // 8, 8, ROWS), axis=0)
+        weighted[...] += jnp.sum((e * value_dots).reshape(count // 8, 8, ROWS), axis=0)
 
     def run(body, low, high):
-        lax.fori_loop(low, high, body, 0, unroll=True)
+        body(low, high)
 
     def shared(i, b):
         take(kv.at[0], s_recv.at[PLACE[i, b]])
@@ -186,14 +186,15 @@
     rows[0:1, :] = inverse
     rows[1:2, :] = jnp.sum(weighted[...], axis=0, keepdims=True) * inverse
 
-    def pass_2(t, carry):
-        n = 15 - t
-        attend = raised[n] * rows[0:1, :]
-        score_grad = (attend * (dots[n] - rows[1:2, :])).astype(BF16)
-        part[n, VALUES] = jnp.dot(attend.astype(BF16), do_n[...], preferred_element_type=F32).astype(BF16)
-        part[n, KEYS] = (jnp.dot(score_grad, q_n[...], preferred_element_type=F32) * INV).astype(BF16)
-        dq_t[...] += jnp.dot(kv[n, KEYS].T, score_grad, preferred_element_type=F32)
-        return carry
+    def pass_2(low, high):
+        count = (high - low) * BLOCK
+        attend = raised[low:high].reshape(count, ROWS) * rows[0:1, :]
+        score_grad = (attend * (dots[low:high].reshape(count, ROWS) - rows[1:2, :])).astype(BF16)
+        value_part = jnp.dot(attend.astype(BF16), do_n[...], preferred_element_type=F32).astype(BF16)
+        key_part = (jnp.dot(score_grad, q_n[...], preferred_element_type=F32) * INV).astype(BF16)
+        part[low:high, VALUES] = value_part.reshape(high - low, BLOCK, D)
+        part[low:high, KEYS] = key_part.reshape(high - low, BLOCK, D)
+        grads[low:high] = score_grad.reshape(high - low, BLOCK, ROWS)
 
     def share(m):
         copy_to(part.at[2 * m + 1], sib_in.at[m], t_send, t_recv.at[m], sibling)
@@ -225,17 +226,24 @@
         take(y_in.at[0], yr_recv.at[which])
         add(i, 0, kind, y_in.at[which, 0], y_in.at[which, 1], y_in.at[which, 2], *more)
 
-    run(pass_2, 0, 1)
+    run(pass_2, 15, 16)
     share(7)
     for m in range(6, -1, -1):
-        run(pass_2, 13 - 2 * m, 15 - 2 * m)
+        run(pass_2, 2 * m + 1, 2 * m + 3)
         share(m)
         settle(*BLOCKS[m + 1])
-        if m == LATE:
+        if BLOCKS[m + 1] == (0, 1):
             gather_y(1, 1, KEYS)
             copy_to(part.at[2 * PLACE[1, 0], KEYS], x_in.at[4], r_send, xr_recv.at[4], beside_x)
-    run(pass_2, 15, 16)
-
+    run(pass_2, 0, 1)
+
+    def query_part(n, carry):
+        some = pl.ds(n * 4, 4)
+        keys_t = kv[some, KEYS].reshape(4 * BLOCK, D).T
+        dq_t[...] += jnp.dot(keys_t, grads[some].reshape(4 * BLOCK, ROWS), preferred_element_type=F32)
+        return carry
+
+    lax.fori_loop(0, 4, query_part, 0)
     for h in range(HEADS):
         cols = slice(h * D, (h + 1) * D)
         unit_rows, scale = unit(q_ref[:, cols].astype(F32))
@@ -278,8 +286,7 @@
         cols = slice(h * D, (h + 1) * D)
         low = (h % 2) * 8 + h // 2
         sums = line_in[low].astype(F32) + line_in[low + 4].astype(F32)
-        unit_rows, scale = unit(k_ref[:, cols].astype(F32))
-        gk_ref[:, cols] = unit_back(sums[KEYS], unit_rows, scale).astype(BF16)
+        gk_ref[:, cols] = unit_back(sums[KEYS], k_unit[h], k_scale[h]).astype(BF16)
         gv_ref[:, cols] = sums[VALUES].astype(BF16)
     take(line_in.at[0 : LINE - 1], l_sem.at[0])
 
@@ -310,10 +317,13 @@
             pltpu.VMEM((ROWS, D), BF16),
             pltpu.VMEM((16, BLOCK, ROWS), F32),
             pltpu.VMEM((16, BLOCK, ROWS), F32),
+            pltpu.VMEM((16, BLOCK, ROWS), BF16),
             pltpu.VMEM((8, ROWS), F32),
             pltpu.VMEM((8, ROWS), F32),
             pltpu.VMEM((8, ROWS), F32),
             pltpu.VMEM((D, ROWS), F32),
+            pltpu.VMEM((HEADS, 16, D), F32),
+            pltpu.VMEM((HEADS, 16, D), F32),
             pltpu.VMEM((HEADS, 2, 16, D), BF16),
             pltpu.VMEM((16, 2, BLOCK, D), BF16),
             pltpu.VMEM((16, 2, BLOCK, D), BF16),
@@ -339,7 +349,7 @@
             dma((2,)),
         ],
         compiler_params=pltpu.CompilerParams(
-            collective_id=0, has_side_effects=True, vmem_limit_bytes=56 * 2**20
+            collective_id=0, has_side_effects=True, vmem_limit_bytes=60 * 2**20
         ),
     )(query_raw, key_raw, values, grad_out)
     return pl.pallas_call(hand_over, out_shape=outs, in_specs=[vmem] * 3, out_specs=[vmem] * 3)(

time: 52.1 us -> 52.1 us (level)
  no operation moved by 1% of the time
where the time goes in v6:
time: 52.1 us; the launch traced here: 51.9 us
  Pallas kernels  51.3 us (98%)
  between operations  0.64 us (1%)
    pallas_call x1, Pallas kernels, shards(): pl.pallas_call(kernel, out_shape=[pltpu.VMEM(a.shape, a.dtype) for a in o...  50.6 us

profile of v6, /device:TPU:1, one launch (start us, length us, event | category | flops | bytes accessed | tf_op | source)
XLA Modules:
  0.0 51.9 jit_solution(14991286803802022053)
XLA Ops:
  0.6 50.6 %shard_map.67 = (bf16[128,1024]{1,0:T(8,128)(2,1)S(1)}, bf16[16,1024]{1,0:T(8,128)(2,1)S(1)}, bf16[16,1024]{1,0:T(8,128)(2,1)S(1)}) custom-call(bf16[128,1024]{1,0:T(8,128)(2,1)} %q_in.1, bf16[16,1024]{1,0:T(8,128)(2,1)} %k_in.1, bf16[16,1024]{1,0:T(8,128)(2,1)} %v_in.1, bf16[128,1024]{1,0:T(8,128)(2,1)} %do_in.1), custom_call_target="tpu_custom_call" | custom-call | tf_op jit(solution)/shard_map/pallas_call | solution.py:304
  51.2 0.7 %shard_map.68 = (bf16[128,1024]{1,0:T(8,128)(2,1)}, bf16[16,1024]{1,0:T(8,128)(2,1)}, bf16[16,1024]{1,0:T(8,128)(2,1)}) custom-call(bf16[128,1024]{1,0:T(8,128)(2,1)S(1)} %get-tuple-element.6.refs_0_, bf16[16,1024]{1,0:T(8,128)(2,1)S(1)} %get-tuple-element.7.refs_1_, bf16[16,1024]{1,0:T(8,128)(2,1)S(1)} %get-tuple-element.8.refs_2_), custom_call_target="tpu_custom_call" | custom-call | tf_op jit(solution)/shard_map/pallas_call | solution.py:355
